TPU v7x, 32 devices: a whole 2x2x4 slice. The times are simulated.
32 devices in a mesh: groups: 2 (over y), seq: 4 (over z), chan: 2 (over x), dp: 2 (over core).
Axes of the slice: x: 2, y: 2, z: 4, core: 2. Of those that a mesh axis runs over, the one named last changes fastest.
Arguments:
- conv_input: bfloat16 [4, 2048, 2048], P(('groups', 'dp'), 'seq', 'chan'), parts along dimension 0, may hold values from -6 to 6
- conv_weight: float32 [4, 2048], P(None, 'chan'), may hold values from -3 to 3
- log_decay: float32 [4, 2048, 32], P(('groups', 'dp'), 'seq', 'chan'), parts along dimension 0, as said below
- state_in: bfloat16 [4, 2048, 128], P(('groups', 'dp'), 'seq'), parts along dimension 0, may hold values from -1.5 to 1.5
- state_out: bfloat16 [4, 2048, 128], P(('groups', 'dp'), 'seq'), parts along dimension 0, may hold values from -1.5 to 1.5
- out_grad: bfloat16 [4, 2048, 2048], P(('groups', 'dp'), 'seq', 'chan'), parts along dimension 0, may hold values from -3 to 3
- lengths: int32 [4], P(('groups', 'dp')), parts along dimension 0, may hold values from 1 to 2048, as said below
- segment_starts: int32 [4, 2], P(('groups', 'dp')), parts along dimension 0, may hold values from 1 to 2047
Outputs:
- input_grad: bfloat16 [4, 2048, 2048], P(('groups', 'dp'), 'seq', 'chan'), parts along dimension 0
- state_in_grad: float32 [4, 2048, 128], P(('groups', 'dp'), 'seq'), parts along dimension 0
- state_out_grad: float32 [4, 2048, 128], P(('groups', 'dp'), 'seq'), parts along dimension 0
- weight_grad: float32 [8, 2048], P('groups', 'chan'), parts along dimension 0
There are 2 independent parts, one for each index of `groups`. A program takes and returns all parts, laid end to end along the dimension named above; an argument that names none is the same for every part. Nothing has to cross between parts.
Inputs may be any that keep to these rules, and one draw needn't show every extreme that they name: `lengths`: at least one series of a group runs the full 2048 steps. `log_decay`: strictly negative.
All inputs are finite; a program needn't handle non-finite values.
Results may differ from a plain program's by a relative error of at most 0.019.
Values may be sent and summed in bfloat16 or wider, within the bound.
A program may use at most 128 MiB of HBM per device.

v0:
```python
import math
import jax
import jax.numpy as jnp
from jax import lax
from jax.sharding import PartitionSpec as P

BLOCK = 256


def shifted(block, axis, distance):
    devices = range(lax.axis_size(axis))
    route = [(i - distance, i) for i in devices if i - distance in devices]
    return lax.ppermute(block, axis, route)


def prefix(part, axis, combine, identity, reverse):
    count = lax.axis_size(axis)
    place = lax.axis_index(axis)
    ahead = count - 1 - place if reverse else place
    gathered = jax.tree.map(lambda a: lax.all_gather(a, axis), part)
    state = jax.tree.map(lambda a, e: jnp.zeros_like(a) + jnp.asarray(e, a.dtype), part, identity)

    def one(hop, state):
        source = count - 1 - hop if reverse else hop
        return combine(
            state, jax.tree.map(lambda a: lax.dynamic_index_in_dim(a, source, 0, False), gathered)
        )

    return lax.fori_loop(0, ahead, one, state)


def block_decay(logs, resets):
    kept = jnp.where(resets[:, :, None], jnp.float32(0.0), logs)
    running = jnp.cumsum(kept, axis=1)
    segment = jnp.cumsum(resets.astype(jnp.int32), axis=1)
    steps = logs.shape[1]
    order = jnp.arange(steps, dtype=jnp.int32)
    final = running[:, -1:, :]
    final_seg = segment[:, -1:]
    start_decay = jnp.where((segment == 0)[:, :, None], jnp.exp(running), jnp.float32(0.0))
    end_decay = jnp.where(
        (segment == final_seg)[:, :, None], jnp.exp(final - running), jnp.float32(0.0)
    )
    whole = jnp.where(final_seg == 0, jnp.exp(final[:, 0, :]), jnp.float32(0.0))
    per_head = jnp.transpose(running, (0, 2, 1))
    spread = per_head[:, :, :, None] - per_head[:, :, None, :]
    linked = (segment[:, :, None] == segment[:, None, :]) & (order[:, None] >= order[None, :])[None]
    linked = linked[:, None]
    decay_map = jnp.where(
        linked, jnp.exp(jnp.where(linked, spread, jnp.float32(0.0))), jnp.float32(0.0)
    )
    return (decay_map, start_decay, end_decay, whole)


def split_pair(values):
    upper = values.astype(jnp.bfloat16)
    lower = (values - upper.astype(jnp.float32)).astype(jnp.bfloat16)
    return (upper, lower)


def pair_product(form, left, right):
    upper, lower = left
    return jnp.einsum(form, upper, right, preferred_element_type=jnp.float32) + jnp.einsum(
        form, lower, right, preferred_element_type=jnp.float32
    )


def block_state(values, matrix, decay):
    scaled = decay[..., None] * values.astype(jnp.float32)
    return pair_product("bshp,bsn->bhpn", split_pair(scaled), matrix)


def compose(earlier, later):
    return (earlier[0] * later[0], later[0][:, :, None, None] * earlier[1] + later[1])


def block_outputs(
    scan_in, masked, in_mat, out_mat, decay_map, start_decay, end_decay, state, grad_state
):
    scores = jnp.einsum("bthp,bshp->bhts", masked, scan_in, preferred_element_type=jnp.float32)
    weighted = (scores * decay_map).astype(jnp.bfloat16)
    inner = jnp.einsum("btn,bsn->bts", out_mat, in_mat, preferred_element_type=jnp.float32)
    carried = (inner[:, None] * decay_map).astype(jnp.bfloat16)
    scaled_grads = start_decay[..., None] * masked.astype(jnp.float32)
    scaled_scan = end_decay[..., None] * scan_in.astype(jnp.float32)
    state_pair = split_pair(state)
    grad_pair = split_pair(grad_state)
    out_part = jnp.einsum("bhts,bsn->btn", weighted, in_mat, preferred_element_type=jnp.float32)
    out_part = out_part + pair_product("bthp,bhpn->btn", split_pair(scaled_grads), state_pair[0])
    out_part = out_part + pair_product("bthp,bhpn->btn", split_pair(scaled_grads), state_pair[1])
    in_part = jnp.einsum("bhrt,brn->btn", weighted, out_mat, preferred_element_type=jnp.float32)
    in_part = in_part + pair_product("bthp,bhpn->btn", split_pair(scaled_scan), grad_pair[0])
    in_part = in_part + pair_product("bthp,bhpn->btn", split_pair(scaled_scan), grad_pair[1])
    scan_grad = jnp.einsum("bhrt,brhp->bthp", carried, masked, preferred_element_type=jnp.float32)
    scan_grad = scan_grad + end_decay[..., None] * pair_product("bhpn,btn->bthp", grad_pair, in_mat)
    return (out_part, in_part, scan_grad)


def backward_conv(padded, weights, count):
    kernel = weights.shape[0]
    summed = jnp.zeros((padded.shape[0], count, padded.shape[2]), jnp.float32)
    for offset in range(kernel):
        start = kernel - 1 - offset
        summed = summed + weights[offset] * padded[:, start : start + count].astype(jnp.float32)
    return summed.astype(jnp.bfloat16)


def per_device(
    conv_input, conv_weight, log_decay, state_in, state_out, out_grad, lengths, segment_starts
):
    batch, local, channels = conv_input.shape
    heads = log_decay.shape[2]
    width = channels // heads
    states = state_in.shape[2]
    kernel = conv_weight.shape[0]
    seq_count = lax.axis_size("seq")
    seq_index = lax.axis_index("seq")
    rim = shifted(conv_input[:, local - (kernel - 1) :, :], "seq", 1)
    padded = jnp.concatenate([rim, conv_input], axis=1)
    mixed = jnp.zeros((batch, local, channels), jnp.float32)
    for offset in range(kernel):
        mixed = mixed + conv_weight[offset] * padded[:, offset : offset + local].astype(jnp.float32)
    position = seq_index * local + jnp.arange(local, dtype=jnp.int32)
    valid = (position[None, :] < lengths[:, None])[:, :, None]
    resets = jnp.any(segment_starts[:, None, :] == position[None, :, None], axis=2)
    gain = jnp.where(resets[:, :, None], jnp.float32(1.0), jnp.sqrt(-jnp.expm1(2.0 * log_decay)))
    sigmoid_u = jax.nn.sigmoid(mixed)
    activated = ((mixed * sigmoid_u).reshape(batch, local, heads, width) * gain[..., None]).reshape(
        batch, local, channels
    )
    scan_in = (
        jnp.where(valid, activated, jnp.float32(0.0))
        .astype(jnp.bfloat16)
        .reshape(batch, local, heads, width)
    )
    masked = jnp.where(valid, out_grad, jnp.zeros_like(out_grad)).reshape(
        batch, local, heads, width
    )
    count = local // BLOCK
    records = []
    carried_decay = jnp.ones((batch, heads), jnp.float32)
    forward_sum = jnp.zeros((batch, heads, width, states), jnp.float32)
    backward_sum = jnp.zeros((batch, heads, width, states), jnp.float32)
    for index in range(count):
        span = slice(index * BLOCK, (index + 1) * BLOCK)
        decay_map, start_decay, end_decay, whole = block_decay(log_decay[:, span], resets[:, span])
        pushed = block_state(scan_in[:, span], state_in[:, span], end_decay)
        pulled = block_state(masked[:, span], state_out[:, span], start_decay)
        records.append((span, decay_map, start_decay, end_decay, whole, pushed, pulled))
        forward_sum = whole[:, :, None, None] * forward_sum + pushed
        carried_decay = carried_decay * whole
    for record in reversed(records):
        backward_sum = record[4][:, :, None, None] * backward_sum + record[6]
    identity = (jnp.ones_like(carried_decay), jnp.zeros_like(forward_sum))
    _, entering = prefix((carried_decay, forward_sum), "seq", compose, identity, False)
    _, leaving = prefix((carried_decay, backward_sum), "seq", compose, identity, True)
    state_now = entering
    entries = []
    for record in records:
        entries.append(state_now)
        state_now = record[4][:, :, None, None] * state_now + record[5]
    grad_now = leaving
    exits = [grad_now] * count
    for index in reversed(range(count)):
        exits[index] = grad_now
        grad_now = records[index][4][:, :, None, None] * grad_now + records[index][6]
    out_list = []
    in_list = []
    scan_list = []
    for index in range(count):
        span, decay_map, start_decay, end_decay, whole, pushed, pulled = records[index]
        out_part, in_part, scan_grad = block_outputs(
            scan_in[:, span],
            masked[:, span],
            state_in[:, span],
            state_out[:, span],
            decay_map,
            start_decay,
            end_decay,
            entries[index],
            exits[index],
        )
        out_list.append(out_part)
        in_list.append(in_part)
        scan_list.append(scan_grad)
    out_local = jnp.concatenate(out_list, axis=1)
    in_local = jnp.concatenate(in_list, axis=1)
    scan_grad = jnp.concatenate(scan_list, axis=1)
    state_in_grad, state_out_grad = (
        lax.psum(in_local.astype(jnp.bfloat16), "chan").astype(jnp.float32),
        lax.psum(out_local.astype(jnp.bfloat16), "chan").astype(jnp.float32),
    )
    slope = sigmoid_u * (1.0 + mixed * (1.0 - sigmoid_u))
    mixed_grad = (scan_grad * gain[..., None]).reshape(batch, local, channels) * slope
    mixed_grad = jnp.where(valid, mixed_grad, jnp.float32(0.0)).astype(jnp.bfloat16)
    after = shifted(mixed_grad[:, : kernel - 1, :], "seq", -1)
    input_grad = backward_conv(jnp.concatenate([mixed_grad, after], axis=1), conv_weight, local)
    wide_grad = mixed_grad.astype(jnp.float32)
    rows = []
    for offset in range(kernel):
        rows.append(
            jnp.sum(wide_grad * padded[:, offset : offset + local].astype(jnp.float32), axis=(0, 1))
        )
    factor = 1.0 / math.sqrt(batch * lax.axis_size("dp") * local * seq_count)
    weight_grad = lax.psum(jnp.stack(rows) * factor, ("seq", "dp"))
    return (input_grad, state_in_grad, state_out_grad, weight_grad)


def solution(mesh):
    placed = (
        P(("groups", "dp"), "seq", "chan"),
        P(None, "chan"),
        P(("groups", "dp"), "seq", "chan"),
        P(("groups", "dp"), "seq", None),
        P(("groups", "dp"), "seq", None),
        P(("groups", "dp"), "seq", "chan"),
        P(("groups", "dp")),
        P(("groups", "dp"), None),
    )
    return jax.shard_map(
        per_device,
        mesh=mesh,
        in_specs=placed,
        out_specs=(
            P(("groups", "dp"), "seq", "chan"),
            P(("groups", "dp"), "seq", None),
            P(("groups", "dp"), "seq", None),
            P("groups", "chan"),
        ),
        check_vma=False,
    )
```

profile of v0, /device:TPU:0, one launch (start us, length us, event | category | flops | bytes accessed | tf_op | source)
XLA Modules:
  0.0 183.1 jit_solution(17551655215464907712)
XLA Ops:
  18.6 1.5 copy.104
  25.3 5.6 %collective-permute-start = (bf16[1,3,1024]{1,2,0:T(8,128)(2,1)}, bf16[1,3,1024]{1,2,0:T(8,128)(2,1)}, u32[]{:S(2)}, u32[]{:S(2)}) collective-permute-start(bf16[1,3,1024]{1,2,0:T(8,128)(2,1)} %copy.122), channel_id=1, source_target_pairs={{0,4},{4,8},{8,12},{1,5},{5,9},{9,13},{2,6},{6,10},{10,14},{3,7},{... | collective-permute-start | bytes 18440 | tf_op jit(solution)/shard_map/ppermute | solution.py:13
  31.0 1.5 copy.123
  32.9 13.7 %all_gather.18 = f32[4,1,16]{2,1,0:T(1,128)} all-gather(f32[1,1,16]{2,1,0:T(1,128)S(1)} %mul.350), channel_id=1, replica_groups=mesh['groups'=2,'seq'=4,'chan'=2,'dp'=2] {'seq'}, dimensions={0}, use_global_device_ids=true | all-gather | bytes 320 | tf_op jit(solution)/shard_map/all_gather | solution.py:20
  51.1 21.5 %all-gather.5.cloned.1.call-done = f32[64,64,128]{2,1,0:T(8,128)} async-done(((f32[16,64,128]{2,1,0:T(8,128)}), f32[64,64,128]{2,1,0:T(8,128)}) %all-gather.5.cloned.1.call-update) | async-done | bytes 2097168 | tf_op jit(solution)/shard_map/all_gather | solution.py:20
  72.6 5.5 %while.26 = (s32[]{:T(128)}, f32[1,16,64,128]{3,2,1,0:T(8,128)S(1)}, s32[]{:T(128)}, f32[4,1,16]{2,1,0:T(1,128)}, f32[4,1,16,64,128]{4,3,2,1,0:T(8,128)}, /*index=5*/s32[]{:T(128)}, s32[]{:T(128)}, s32[]{:T(128)}, s32[]{:T(128)}) while((s32[]{:T(128)}, f32[1,16,64,128]{3,2,1,0:T(8,128)S(1)}, s32[]{:T(128)}, f32[4,1,16]{2,1,0:T(1,128)}, ...), condition=%wide.region_10.11_spmd, body=%wide.region_9.10_spmd.sunk | while | flops 262150 | bytes 1573203 | solution.py:29
  73.2 1.2 bitcast_add_fusion.12
  75.0 1.2 bitcast_add_fusion.12
  76.9 1.2 bitcast_add_fusion.12
  79.8 1.3 fusion.34
  81.2 1.3 fusion.35
  82.6 6.2 %fusion.12 = (f32[1024]{0:T(1024)S(1)}, f32[1024]{0:T(1024)S(1)}, f32[1024]{0:T(1024)S(1)}, f32[1024]{0:T(1024)S(1)}, bf16[1,512,1024]{1,2,0:T(8,128)(2,1)}, /*index=5*/f32[1,512,1024]{1,2,0:T(8,128)S(1)}) fusion(bf16[1,512,1024]{1,2,0:T(8,128)(2,1)S(1)} %copy.123, bf16[1,3,1024]{1,2,0:T(8,128)(2,1)} %collective-permute-done, ...), kind=kLoop, calls=%fused_computation.35 | loop fusion | flops 25686016 | bytes 6363648 | tf_op jit(solution)/shard_map/reduce_sum | solution.py:202
  91.7 1.7 slice.175
  93.3 1.3 collective-permute-start.1
  94.7 40.0 %psum.23 = f32[4,1024]{1,0:T(4,128)} all-reduce(f32[4,1024]{1,0:T(4,128)S(1)} %maximum_multiply_fusion), channel_id=1, replica_groups=mesh['groups'=2,'seq'=4,'chan'=2,'dp'=2] {'seq','dp'}, use_global_device_ids=true, to_apply=%region_21.22 | all-reduce | flops 4096 | bytes 32768 | tf_op jit(solution)/shard_map/psum | solution.py:205
  134.6 1.4 convolution_bitcast_fusion.14
  136.1 1.6 convolution_bitcast_fusion.12
  138.4 1.6 convert_reduce_fusion.1
  141.7 1.6 convert_reduce_fusion
  149.2 3.9 %fusion.11 = bf16[1,512,1024]{1,2,0:T(8,128)(2,1)S(1)} fusion(bf16[1,512,1024]{1,2,0:T(8,128)(2,1)S(1)} %copy-done, bf16[1,3,1024]{1,2,0:T(8,128)(2,1)} %collective-permute-done.1, f32[1024]{0:T(1024)S(1)} %bitcast.442, f32[1024]{0:T(1024)S(1)} %bitcast.444, f32[1024]{0:T(1024)S(1)} %bitcast.440, f32[1024]{0:T(1024)S(1)} %bitcast.438), kind=kLoop, calls=%fused_computation.34 | loop fusion | flops 11010048 | bytes 2119680 | tf_op jit(solution)/shard_map/convert_element_type | solution.py:105
  153.1 1.3 copy.126
  154.4 19.0 %all-reduce.3.cloned.1.call-done = (bf16[1,512,128]{2,1,0:T(8,128)(2,1)}, bf16[1,512,128]{2,1,0:T(8,128)(2,1)}) async-done(((bf16[1,512,128]{2,1,0:T(8,128)(2,1)}, bf16[1,512,128]{2,1,0:T(8,128)(2,1)}), (bf16[1,512,128]{2,1,0:T(8,128)(2,1)}, bf16[1,512,128]{2,1,0:T(8,128)(2,1)})) %all-reduce.3.cloned.1.call-update) | async-done | bytes 262160 | tf_op jit(solution)/shard_map/psum | solution.py:190
  173.3 1.6 convert_element_type.247
  175.0 1.6 convert_element_type.254
  (208 shorter events, 32.2 us)
Async XLA Ops:
  7.2 65.4 %all-gather.5.cloned.1.call-start = ((), (), s32[]{:S(2)}) async-start(), calls=%async_computation | async-start | bytes 2621440 | tf_op jit(solution)/shard_map/all_gather | solution.py:20
  13.6 4.9 %copy-start.31 = (s32[256]{0:T(256)}, s32[256]{0:T(256)S(1)}, u32[]{:S(2)}) copy-start(s32[256]{0:T(256)S(1)} %get-tuple-element.233) | copy-start | bytes 3076
  17.9 2.7 %copy-start.9 = (f32[1,256,16]{1,2,0:T(8,128)}, f32[1,256,16]{1,2,0:T(8,128)S(1)}, u32[]{:S(2)}) copy-start(f32[1,256,16]{1,2,0:T(8,128)S(1)} %copy.155) | copy-start | bytes 49156
  18.6 1.6 copy-start.41
  23.6 23.0 %copy-start.30 = (f32[4,1024]{1,0:T(4,128)S(1)}, f32[4,1024]{1,0:T(4,128)}, u32[]{:S(2)}) copy-start(f32[4,1024]{1,0:T(4,128)} %param.13) | copy-start | bytes 49156
  23.6 24.8 %copy-start.13 = (f32[1,512,16]{1,2,0:T(8,128)S(1)}, f32[1,512,16]{1,2,0:T(8,128)}, u32[]{:S(2)}) copy-start(f32[1,512,16]{1,2,0:T(8,128)} %param.14) | copy-start | bytes 98308
  23.6 24.8 %copy-start.36 = (pred[512]{0:T(512)(128)(4,1)S(1)}, pred[512]{0:T(512)(128)(4,1)}, u32[]{:S(2)}) copy-start(pred[512]{0:T(512)(128)(4,1)} %copy-done.35) | copy-start | bytes 1540
  23.6 24.8 %copy-start.32 = (s32[256]{0:T(256)S(1)}, s32[256]{0:T(256)}, u32[]{:S(2)}) copy-start(s32[256]{0:T(256)} %copy-done.31) | copy-start | bytes 3076
  23.6 25.6 %copy-start.34 = (s32[256]{0:T(256)S(1)}, s32[256]{0:T(256)}, u32[]{:S(2)}) copy-start(s32[256]{0:T(256)} %copy-done.33) | copy-start | bytes 3076
  23.6 25.7 %copy-start.3 = (bf16[1,512,128]{2,1,0:T(8,128)(2,1)S(1)}, bf16[1,512,128]{2,1,0:T(8,128)(2,1)}, u32[]{:S(2)}) copy-start(bf16[1,512,128]{2,1,0:T(8,128)(2,1)} %param.15) | copy-start | bytes 393220
  23.6 120.6 %all-gather.7.cloned.1.call-start = ((), (), s32[]{:S(2)}) async-start(), calls=%async_computation.1 | async-start | bytes 2621440 | tf_op jit(solution)/shard_map/all_gather | solution.py:20
  25.3 57.2 %collective-permute-start = (bf16[1,3,1024]{1,2,0:T(8,128)(2,1)}, bf16[1,3,1024]{1,2,0:T(8,128)(2,1)}, u32[]{:S(2)}, u32[]{:S(2)}) collective-permute-start(bf16[1,3,1024]{1,2,0:T(8,128)(2,1)} %copy.122), channel_id=1, source_target_pairs={{0,4},{4,8},{8,12},{1,5},{5,9},{9,13},{2,6},{6,10},{10,14},{3,7},{... | collective-permute-start | bytes 18440 | tf_op jit(solution)/shard_map/ppermute | solution.py:13
  49.3 31.9 %copy-start.14 = (pred[256,256]{1,0:T(8,128)(4,1)}, pred[256,256]{1,0:T(8,128)(4,1)S(1)}, u32[]{:S(2)}) copy-start(pred[256,256]{1,0:T(8,128)(4,1)S(1)} %fusion.110) | copy-start | bytes 196612
  72.6 5.8 %copy-start.39 = (f32[16]{0:T(128)S(1)}, f32[16]{0:T(128)}, u32[]{:S(2)}) copy-start(f32[16]{0:T(128)} %get-tuple-element.255) | copy-start | bytes 196
  91.6 81.7 %all-reduce.3.cloned.1.call-start = ((), (), s32[]{:S(2)}) async-start(), calls=%async_computation.2 | async-start | bytes 524288 | tf_op jit(solution)/shard_map/psum | solution.py:190
  93.3 55.8 %collective-permute-start.1 = (bf16[1,3,1024]{1,2,0:T(8,128)(2,1)}, bf16[1,3,1024]{1,2,0:T(8,128)(2,1)}, u32[]{:S(2)}, u32[]{:S(2)}) collective-permute-start(bf16[1,3,1024]{1,2,0:T(8,128)(2,1)} %slice.175), channel_id=1, source_target_pairs={{4,0},{8,4},{12,8},{5,1},{9,5},{13,9},{6,2},{10,6},{14,10},{7,3},{... | collective-permute-start | bytes 18440 | tf_op jit(solution)/shard_map/ppermute | solution.py:13
  134.6 3.1 %copy-start.2 = (f32[1,16,64,128]{3,2,1,0:T(8,128)S(1)}, f32[1,16,64,128]{3,2,1,0:T(8,128)}, u32[]{:S(2)}) copy-start(f32[1,16,64,128]{3,2,1,0:T(8,128)} %copy-done.1) | copy-start | bytes 1572868
  136.1 2.3 %copy-start.17 = (pred[256,256]{1,0:T(8,128)(4,1)S(1)}, pred[256,256]{1,0:T(8,128)(4,1)}, u32[]{:S(2)}) copy-start(pred[256,256]{1,0:T(8,128)(4,1)} %fusion.111) | copy-start | bytes 196612
  136.1 2.3 %copy-start.29 = (f32[16,256]{1,0:T(8,128)S(1)}, f32[16,256]{1,0:T(8,128)}, u32[]{:S(2)}) copy-start(f32[16,256]{1,0:T(8,128)} %bitcast_add_fusion.5) | copy-start | bytes 49156
  147.3 1.8 copy-start
  147.3 1.8 copy-start.19
  147.3 1.8 copy-start.21
  147.3 1.8 copy-start.23
  147.3 1.8 copy-start.25
  (25 other events, 28.1 us)
Sparse Core Ops, SparseCore 0:
  23.7 48.7 all-gather.4
  91.7 46.4 all-gather.6
  149.2 24.0 all-reduce.2
where the time goes:
time: 184 us; the launch traced here: 183 us
  blocking collectives  53.6 us (29%)
  waiting for transfers between devices  40.5 us (22%)
  other arithmetic  26.6 us (14%)
  matrix products  21.6 us (12%)
  between operations  18 us (10%)
  local copies, waits for them, and re-layouts  15.7 us (9%)
  starting transfers between devices  7.02 us (4%)
    psum x1, blocking collectives, per_device(): weight_grad = lax.psum(jnp.stack(rows) * factor, ('seq', 'dp'))  40 us
    all_gather x2, waiting for transfers between devices, prefix(): gathered = jax.tree.map(lambda a: lax.all_gather(a, axis), part)  21.5 us
    psum x1, waiting for transfers between devices, per_device(): lax.psum(in_local.astype(jnp.bfloat16), 'chan').astype(jnp.float32)  19 us
    all_gather x1, blocking collectives, prefix(): gathered = jax.tree.map(lambda a: lax.all_gather(a, axis), part)  13.7 us
    dot_general x14, matrix products, pair_product(): jnp.einsum(form, lower, right, preferred_element_type=jnp.float32)  8.56 us
    ppermute x2, starting transfers between devices, shifted(): return lax.ppermute(block, axis, route)  6.9 us
    reduce_sum x1, other arithmetic, per_device(): jnp.sum(wide_grad * padded[:, offset:offset + local].astype(jnp.float32),...  6.22 us
    unnamed x95, local copies, waits for them, and re-layouts  6.05 us
  transfers between devices with their start and end apart: 5, of which 2 were waited for; matrix products, arithmetic and copies ran while one was open for 21% of the time, Pallas kernels for 0%

commit v1 on v0

--- a/solution.py
+++ b/solution.py
@@ -202,7 +202,7 @@
             jnp.sum(wide_grad * padded[:, offset : offset + local].astype(jnp.float32), axis=(0, 1))
         )
     factor = 1.0 / math.sqrt(batch * lax.axis_size("dp") * local * seq_count)
-    weight_grad = lax.psum(jnp.stack(rows) * factor, ("seq", "dp"))
+    weight_grad = jnp.sum(lax.all_gather(jnp.stack(rows) * factor, axis_name=("seq", "dp")), axis=0)
     return (input_grad, state_in_grad, state_out_grad, weight_grad)
 
 

time: 184 us -> 179 us (0.973)
  blocking collectives: 53.6 us -> 41.3 us
  waiting for transfers between devices: 40.5 us -> 47.2 us
    psum x1 -> x0, blocking collectives: 40 us -> none  [per_device(): weight_grad = lax.psum(jnp.stack(rows) * factor, ('seq', 'dp'))]
    all_gather x0 -> x1, blocking collectives: none -> 27.7 us  [per_device(): lax.all_gather(jnp.stack(rows) * factor, axis_name=('seq', 'dp'))]
    all_gather x2, waiting for transfers between devices: 21.5 us -> 27.4 us  [prefix(): gathered = jax.tree.map(lambda a: lax.all_gather(a, axis), part)]
    unnamed x95 -> x99, local copies, waits for them, and re-layouts: 6.05 us -> 6.05 us
  transfers between devices with their start and end apart: 5 -> 5, of which waited for: 2 -> 3; matrix products, arithmetic and copies ran while one was open for 21% -> 21% of each run, Pallas kernels for 0% -> 0%
where the time goes in v1:
time: 179 us; the launch traced here: 178 us
  waiting for transfers between devices  47.2 us (26%)
  blocking collectives  41.3 us (23%)
  other arithmetic  27.2 us (15%)
  matrix products  21.6 us (12%)
  between operations  18 us (10%)
  local copies, waits for them, and re-layouts  15.6 us (9%)
  starting transfers between devices  7.04 us (4%)
    all_gather x1, blocking collectives, per_device(): lax.all_gather(jnp.stack(rows) * factor, axis_name=('seq', 'dp'))  27.7 us
    all_gather x2, waiting for transfers between devices, prefix(): gathered = jax.tree.map(lambda a: lax.all_gather(a, axis), part)  27.4 us
    psum x1, waiting for transfers between devices, per_device(): lax.psum(in_local.astype(jnp.bfloat16), 'chan').astype(jnp.float32)  19.8 us
    all_gather x1, blocking collectives, prefix(): gathered = jax.tree.map(lambda a: lax.all_gather(a, axis), part)  13.7 us
    dot_general x14, matrix products, pair_product(): jnp.einsum(form, lower, right, preferred_element_type=jnp.float32)  8.59 us
    ppermute x2, starting transfers between devices, shifted(): return lax.ppermute(block, axis, route)  6.92 us
    reduce_sum x1, other arithmetic, per_device(): jnp.sum(wide_grad * padded[:, offset:offset + local].astype(jnp.float32),...  6.22 us
    unnamed x99, local copies, waits for them, and re-layouts  6.05 us
  transfers between devices with their start and end apart: 5, of which 3 were waited for; matrix products, arithmetic and copies ran while one was open for 21% of the time, Pallas kernels for 0%

profile of v1, /device:TPU:0, one launch (start us, length us, event | category | flops | bytes accessed | tf_op | source)
XLA Modules:
  0.0 178.2 jit_solution(10396637352771961481)
XLA Ops:
  18.6 1.5 copy.104
  25.3 5.6 %collective-permute-start = (bf16[1,3,1024]{1,2,0:T(8,128)(2,1)}, bf16[1,3,1024]{1,2,0:T(8,128)(2,1)}, u32[]{:S(2)}, u32[]{:S(2)}) collective-permute-start(bf16[1,3,1024]{1,2,0:T(8,128)(2,1)} %copy.122), channel_id=1, source_target_pairs={{0,4},{4,8},{8,12},{1,5},{5,9},{9,13},{2,6},{6,10},{10,14},{3,7},{... | collective-permute-start | bytes 18440 | tf_op jit(solution)/shard_map/ppermute | solution.py:13
  31.0 1.5 copy.123
  32.9 13.7 %all_gather.22 = f32[4,1,16]{2,1,0:T(1,128)} all-gather(f32[1,1,16]{2,1,0:T(1,128)S(1)} %mul.357), channel_id=1, replica_groups=mesh['groups'=2,'seq'=4,'chan'=2,'dp'=2] {'seq'}, dimensions={0}, use_global_device_ids=true | all-gather | bytes 320 | tf_op jit(solution)/shard_map/all_gather | solution.py:20
  51.1 21.5 %all-gather.5.cloned.1.call-done = f32[64,64,128]{2,1,0:T(8,128)} async-done(((f32[16,64,128]{2,1,0:T(8,128)}), f32[64,64,128]{2,1,0:T(8,128)}) %all-gather.5.cloned.1.call-update) | async-done | bytes 2097168 | tf_op jit(solution)/shard_map/all_gather | solution.py:20
  72.6 5.5 %while.26 = (s32[]{:T(128)}, f32[1,16,64,128]{3,2,1,0:T(8,128)S(1)}, s32[]{:T(128)}, f32[4,1,16]{2,1,0:T(1,128)}, f32[4,1,16,64,128]{4,3,2,1,0:T(8,128)}, /*index=5*/s32[]{:T(128)}, s32[]{:T(128)}, s32[]{:T(128)}, s32[]{:T(128)}) while((s32[]{:T(128)}, f32[1,16,64,128]{3,2,1,0:T(8,128)S(1)}, s32[]{:T(128)}, f32[4,1,16]{2,1,0:T(1,128)}, ...), condition=%wide.region_10.11_spmd, body=%wide.region_9.10_spmd.sunk | while | flops 262150 | bytes 1573203 | solution.py:29
  73.2 1.2 bitcast_add_fusion.12
  75.0 1.2 bitcast_add_fusion.12
  79.8 1.3 fusion.34
  81.2 1.3 fusion.35
  82.6 6.2 %fusion.12 = (f32[1024]{0:T(1024)S(1)}, f32[1024]{0:T(1024)S(1)}, f32[1024]{0:T(1024)S(1)}, f32[1024]{0:T(1024)S(1)}, bf16[1,512,1024]{1,2,0:T(8,128)(2,1)}, /*index=5*/f32[1,512,1024]{1,2,0:T(8,128)S(1)}) fusion(bf16[1,512,1024]{1,2,0:T(8,128)(2,1)S(1)} %copy.123, bf16[1,3,1024]{1,2,0:T(8,128)(2,1)} %collective-permute-done, ...), kind=kLoop, calls=%fused_computation.35 | loop fusion | flops 25686016 | bytes 6363648 | tf_op jit(solution)/shard_map/reduce_sum | solution.py:202
  91.6 1.7 slice.175
  93.3 1.3 collective-permute-start.1
  94.6 27.7 %all_gather.27 = f32[8,4,1024]{2,1,0:T(4,128)S(1)} all-gather(f32[1,4,1024]{2,1,0:T(4,128)S(1)} %maximum_multiply_fusion), channel_id=1, replica_groups=mesh['groups'=2,'seq'=4,'chan'=2,'dp'=2] {'seq','dp'}, dimensions={0}, use_global_device_ids=true | all-gather | bytes 147456 | tf_op jit(solution)/shard_map/all_gather | solution.py:205
  122.9 1.5 convolution_bitcast_fusion.14
  124.4 1.6 convolution_bitcast_fusion.12
  126.7 1.6 convert_reduce_fusion.1
  130.1 1.6 convert_reduce_fusion
  132.6 6.0 %all-gather.7.cloned.1.call-done = f32[64,64,128]{2,1,0:T(8,128)} async-done(((f32[16,64,128]{2,1,0:T(8,128)}), f32[64,64,128]{2,1,0:T(8,128)}) %all-gather.7.cloned.1.call-update) | async-done | bytes 2097168 | tf_op jit(solution)/shard_map/all_gather | solution.py:20
  143.5 3.9 %fusion.11 = bf16[1,512,1024]{1,2,0:T(8,128)(2,1)S(1)} fusion(bf16[1,512,1024]{1,2,0:T(8,128)(2,1)S(1)} %copy-done, bf16[1,3,1024]{1,2,0:T(8,128)(2,1)} %collective-permute-done.1, f32[1024]{0:T(1024)S(1)} %bitcast.442, f32[1024]{0:T(1024)S(1)} %bitcast.444, f32[1024]{0:T(1024)S(1)} %bitcast.440, f32[1024]{0:T(1024)S(1)} %bitcast.438), kind=kLoop, calls=%fused_computation.34 | loop fusion | flops 11010048 | bytes 2119680 | tf_op jit(solution)/shard_map/convert_element_type | solution.py:105
  147.4 1.3 copy.126
  148.7 19.8 %all-reduce.3.cloned.1.call-done = (bf16[1,512,128]{2,1,0:T(8,128)(2,1)}, bf16[1,512,128]{2,1,0:T(8,128)(2,1)}) async-done(((bf16[1,512,128]{2,1,0:T(8,128)(2,1)}, bf16[1,512,128]{2,1,0:T(8,128)(2,1)}), (bf16[1,512,128]{2,1,0:T(8,128)(2,1)}, bf16[1,512,128]{2,1,0:T(8,128)(2,1)})) %all-reduce.3.cloned.1.call-update) | async-done | bytes 262160 | tf_op jit(solution)/shard_map/psum | solution.py:190
  168.4 1.6 convert_element_type.247
  170.1 1.6 convert_element_type.254
  (213 shorter events, 33.9 us)
Async XLA Ops:
  7.2 65.4 %all-gather.5.cloned.1.call-start = ((), (), s32[]{:S(2)}) async-start(), calls=%async_computation | async-start | bytes 2621440 | tf_op jit(solution)/shard_map/all_gather | solution.py:20
  13.6 4.9 %copy-start.33 = (s32[256]{0:T(256)}, s32[256]{0:T(256)S(1)}, u32[]{:S(2)}) copy-start(s32[256]{0:T(256)S(1)} %get-tuple-element.233) | copy-start | bytes 3076
  17.9 2.7 %copy-start.11 = (f32[1,256,16]{1,2,0:T(8,128)}, f32[1,256,16]{1,2,0:T(8,128)S(1)}, u32[]{:S(2)}) copy-start(f32[1,256,16]{1,2,0:T(8,128)S(1)} %copy.156) | copy-start | bytes 49156
  23.6 23.0 %copy-start.32 = (f32[4,1024]{1,0:T(4,128)S(1)}, f32[4,1024]{1,0:T(4,128)}, u32[]{:S(2)}) copy-start(f32[4,1024]{1,0:T(4,128)} %param.13) | copy-start | bytes 49156
  23.6 24.8 %copy-start.15 = (f32[1,512,16]{1,2,0:T(8,128)S(1)}, f32[1,512,16]{1,2,0:T(8,128)}, u32[]{:S(2)}) copy-start(f32[1,512,16]{1,2,0:T(8,128)} %param.14) | copy-start | bytes 98308
  23.6 24.8 %copy-start.38 = (pred[512]{0:T(512)(128)(4,1)S(1)}, pred[512]{0:T(512)(128)(4,1)}, u32[]{:S(2)}) copy-start(pred[512]{0:T(512)(128)(4,1)} %copy-done.37) | copy-start | bytes 1540
  23.6 24.8 %copy-start.34 = (s32[256]{0:T(256)S(1)}, s32[256]{0:T(256)}, u32[]{:S(2)}) copy-start(s32[256]{0:T(256)} %copy-done.33) | copy-start | bytes 3076
  23.6 25.6 %copy-start.36 = (s32[256]{0:T(256)S(1)}, s32[256]{0:T(256)}, u32[]{:S(2)}) copy-start(s32[256]{0:T(256)} %copy-done.35) | copy-start | bytes 3076
  23.6 25.7 %copy-start.3 = (bf16[1,512,128]{2,1,0:T(8,128)(2,1)S(1)}, bf16[1,512,128]{2,1,0:T(8,128)(2,1)}, u32[]{:S(2)}) copy-start(bf16[1,512,128]{2,1,0:T(8,128)(2,1)} %param.15) | copy-start | bytes 393220
  23.6 114.9 %all-gather.7.cloned.1.call-start = ((), (), s32[]{:S(2)}) async-start(), calls=%async_computation.1 | async-start | bytes 2621440 | tf_op jit(solution)/shard_map/all_gather | solution.py:20
  25.3 57.2 %collective-permute-start = (bf16[1,3,1024]{1,2,0:T(8,128)(2,1)}, bf16[1,3,1024]{1,2,0:T(8,128)(2,1)}, u32[]{:S(2)}, u32[]{:S(2)}) collective-permute-start(bf16[1,3,1024]{1,2,0:T(8,128)(2,1)} %copy.122), channel_id=1, source_target_pairs={{0,4},{4,8},{8,12},{1,5},{5,9},{9,13},{2,6},{6,10},{10,14},{3,7},{... | collective-permute-start | bytes 18440 | tf_op jit(solution)/shard_map/ppermute | solution.py:13
  32.8 57.3 %copy-start.7 = (f32[1,256,16]{1,2,0:T(8,128)}, f32[1,256,16]{1,2,0:T(8,128)S(1)}, u32[]{:S(2)}) copy-start(f32[1,256,16]{1,2,0:T(8,128)S(1)} %copy.157) | copy-start | bytes 49156
  49.3 31.8 %copy-start.16 = (pred[256,256]{1,0:T(8,128)(4,1)}, pred[256,256]{1,0:T(8,128)(4,1)S(1)}, u32[]{:S(2)}) copy-start(pred[256,256]{1,0:T(8,128)(4,1)S(1)} %fusion.110) | copy-start | bytes 196612
  72.6 5.8 %copy-start.41 = (f32[16]{0:T(128)S(1)}, f32[16]{0:T(128)}, u32[]{:S(2)}) copy-start(f32[16]{0:T(128)} %get-tuple-element.255) | copy-start | bytes 196
  91.6 76.9 %all-reduce.3.cloned.1.call-start = ((), (), s32[]{:S(2)}) async-start(), calls=%async_computation.2 | async-start | bytes 524288 | tf_op jit(solution)/shard_map/psum | solution.py:190
  93.3 50.1 %collective-permute-start.1 = (bf16[1,3,1024]{1,2,0:T(8,128)(2,1)}, bf16[1,3,1024]{1,2,0:T(8,128)(2,1)}, u32[]{:S(2)}, u32[]{:S(2)}) collective-permute-start(bf16[1,3,1024]{1,2,0:T(8,128)(2,1)} %slice.175), channel_id=1, source_target_pairs={{4,0},{8,4},{12,8},{5,1},{9,5},{13,9},{6,2},{10,6},{14,10},{7,3},{... | collective-permute-start | bytes 18440 | tf_op jit(solution)/shard_map/ppermute | solution.py:13
  122.9 3.1 %copy-start.2 = (f32[1,16,64,128]{3,2,1,0:T(8,128)S(1)}, f32[1,16,64,128]{3,2,1,0:T(8,128)}, u32[]{:S(2)}) copy-start(f32[1,16,64,128]{3,2,1,0:T(8,128)} %copy-done.1) | copy-start | bytes 1572868
  122.9 3.1 %copy-start.8 = (f32[1,256,16]{1,2,0:T(8,128)S(1)}, f32[1,256,16]{1,2,0:T(8,128)}, u32[]{:S(2)}) copy-start(f32[1,256,16]{1,2,0:T(8,128)} %copy-done.7) | copy-start | bytes 49156
  124.4 2.3 %copy-start.19 = (pred[256,256]{1,0:T(8,128)(4,1)S(1)}, pred[256,256]{1,0:T(8,128)(4,1)}, u32[]{:S(2)}) copy-start(pred[256,256]{1,0:T(8,128)(4,1)} %fusion.111) | copy-start | bytes 196612
  124.4 2.3 %copy-start.31 = (f32[16,256]{1,0:T(8,128)S(1)}, f32[16,256]{1,0:T(8,128)}, u32[]{:S(2)}) copy-start(f32[16,256]{1,0:T(8,128)} %bitcast_add_fusion.5) | copy-start | bytes 49156
  131.7 6.9 %copy-start.5 = (bf16[256,256]{1,0:T(8,128)(2,1)}, bf16[256,256]{1,0:T(8,128)(2,1)S(1)}, u32[]{:S(2)}) copy-start(bf16[256,256]{1,0:T(8,128)(2,1)S(1)} %convert_reduce_fusion) | copy-start | bytes 393220
  141.6 1.8 %copy-start = (bf16[1,512,1024]{1,2,0:T(8,128)(2,1)S(1)}, bf16[1,512,1024]{1,2,0:T(8,128)(2,1)}, u32[]{:S(2)}) copy-start(bf16[1,512,1024]{1,2,0:T(8,128)(2,1)} %get-tuple-element.228) | copy-start | bytes 3145732
  141.6 1.8 %copy-start.21 = (f32[1,1024]{1,0:T(1,128)S(1)}, f32[1,1024]{1,0:T(1,128)}, u32[]{:S(2)}) copy-start(f32[1,1024]{1,0:T(1,128)} %get-tuple-element.244) | copy-start | bytes 12292
  141.6 1.8 %copy-start.23 = (f32[1,1024]{1,0:T(1,128)S(1)}, f32[1,1024]{1,0:T(1,128)}, u32[]{:S(2)}) copy-start(f32[1,1024]{1,0:T(1,128)} %get-tuple-element.245) | copy-start | bytes 12292
  (27 other events, 32.5 us)
Sparse Core Ops, SparseCore 0:
  23.7 48.7 all-gather.4
  91.7 46.8 all-gather.6
  143.5 24.8 all-reduce.2
